TPU v7x, 32 devices: a whole 2x2x4 slice. The times are simulated.
32 devices in a mesh: dp: 2 (over core), expert: 16 (over z, y, x).
Axes of the slice: x: 2, y: 2, z: 4, core: 2. Of those that a mesh axis runs over, the one named last changes fastest.
Arguments:
- hidden_saved: bfloat16 [2, 16, 448, 1024], P('dp', 'expert'), may hold values from -6 to 6
- down_weight: bfloat16 [16, 1024, 3584], P('expert', 'dp'), may hold values from -0.1875 to 0.1875
- route_device: int32 [4096, 4], P(('dp', 'expert')), may hold values from 0 to 15, all different within a row; in each aligned block of 128 rows (0 to 127, 128 to 255, ...) at most 40 rows name the same one
- replica_flag: int32 [4096, 4], P(('dp', 'expert')), may hold values 0 or 1
- gate_values: float32 [4096, 4], P(('dp', 'expert')), may hold values from 0.05 to 1
- grad_out: bfloat16 [4096, 3584], P(('dp', 'expert')), may hold values from -6 to 6
Outputs:
- layer_out: bfloat16 [4096, 3584], P(('dp', 'expert'))
- grad_hidden: bfloat16 [2, 16, 448, 1024], P('dp', 'expert')
- grad_weight: bfloat16 [16, 1024, 3584], P('expert', 'dp')
Inputs may be any that keep to these rules, and one draw needn't show every extreme that they name: `route_device`: the 4 numbers of a row differ; the rows of one device name any one device at most 40 times, and some device exactly 40 times.
All inputs are finite; a program needn't handle non-finite values. No bound on the sum of `replica_flag` on one device may be relied on, other than what follows from the above.
Results may differ from a plain program's by a relative error of at most 0.012.
Values may be sent and summed in bfloat16 or wider, within the bound.
No kernel may reach another device: no remote copies, remote signals or barrier semaphores. Data moves between devices by JAX's collectives and lax.ppermute only.
A program may use at most 192 MiB of HBM per device.

v0:
```python
import functools
import jax
import jax.numpy as jnp
from jax import lax
from jax.experimental import pallas as pl
from jax.experimental.pallas import tpu as pltpu
from jax.sharding import PartitionSpec as P

F32, BF16, I32 = jnp.float32, jnp.bfloat16, jnp.int32
LANES = 128
VMEM_LIMIT = 40 * 1024 * 1024


def swapped(value, axis, distance):
    count = lax.axis_size(axis)
    pairs = [(source, (source + distance) % count) for source in range(count)]
    return lax.ppermute(value, axis, pairs)


def dot(left, right, left_dim=1, right_dim=0):
    contract = (((left_dim,), (right_dim,)), ((), ()))
    return lax.dot_general(left, right, contract, preferred_element_type=F32)


def iota(shape, dim):
    return lax.broadcasted_iota(I32, shape, dim).astype(F32)


def row_of(rows, cap, lanes):
    row = iota((rows, lanes), 0)
    group = jnp.floor((row + 0.5) * (1.0 / cap))
    return group, row - group * cap


def before_mask(size):
    return (iota((size, size), 0) < iota((size, size), 1)).astype(BF16)


def call(body, grid, in_specs, out_specs, out_shape, scratch, *operands):
    return pl.pallas_call(
        body,
        grid=(grid,),
        in_specs=in_specs,
        out_specs=out_specs,
        out_shape=out_shape,
        scratch_shapes=scratch,
        compiler_params=pltpu.CompilerParams(vmem_limit_bytes=VMEM_LIMIT),
        cost_estimate=pl.CostEstimate(flops=0, bytes_accessed=0, transcendentals=0),
    )(*operands)


def whole_block(shape):
    return pl.BlockSpec(shape, lambda step: (0,) * len(shape))


def columns(rows, tile):
    return pl.BlockSpec((rows, tile), lambda step: (0, step))


def pack_kernel(cap, top, half, mirrored, meta_ref, tokens_ref, packed_ref, mix_ref, sel_ref, gate_ref):
    rows, tok = sel_ref.shape

    @pl.when(pl.program_id(0) == 0)
    def _():
        me = lax.axis_index("expert")
        source = lax.rem(me + half, 2 * half) if mirrored else 0
        first = (lax.div(me, half) * half).astype(F32)
        row = meta_ref[pl.ds(source, 1), :]
        dest = iota((LANES, tok), 0)
        inside = dest < half
        dest = dest + first
        hit = jnp.zeros((LANES, tok), F32)
        gate = jnp.zeros((LANES, tok), F32)
        for k in range(top):
            device = jnp.floor(row[:, k * tok : (k + 1) * tok] * 0.5)
            named = (dest == device) & inside
            hit = jnp.where(named, 1.0, hit)
            gate = jnp.where(named, row[:, (top + k) * tok : (top + k + 1) * tok], gate)
        place = dot(hit.astype(BF16), before_mask(tok))
        place = jnp.where(hit > 0.5, place, -1.0).astype(BF16)
        group, at = row_of(rows, cap, LANES)
        spread = (iota((rows, LANES), 1) == group).astype(BF16)
        chosen = dot(spread, place) == at
        high = gate.astype(BF16)
        rest = gate - high.astype(F32)
        mid = rest.astype(BF16)
        low = (rest - mid.astype(F32)).astype(BF16)
        high, mid, low = dot(spread, high), dot(spread, mid), dot(spread, low)
        none = jnp.zeros((rows, tok), F32)
        sel_ref[...] = jnp.where(chosen, 1.0, none).astype(BF16)
        scale = jnp.sum(jnp.where(chosen, high + mid + low, none), axis=1, keepdims=True)
        gate_ref[...] = jnp.broadcast_to(scale, (rows, LANES))
        mix_ref[:, :tok] = jnp.where(chosen, high, none).astype(BF16)
        mix_ref[:, tok:] = jnp.where(chosen, mid, none).astype(BF16)

    packed = dot(sel_ref[...], tokens_ref[...]) * gate_ref[:, :1]
    packed_ref[...] = packed.astype(BF16)


def pack(meta, tokens, cap, top, half, mirrored, tile):
    tok, width = tokens.shape
    rows = half * cap
    return call(
        functools.partial(pack_kernel, cap, top, half, mirrored),
        width // tile,
        [whole_block(meta.shape), columns(tok, tile)],
        [columns(rows, tile), whole_block((rows, 2 * tok))],
        [jax.ShapeDtypeStruct((rows, width), BF16), jax.ShapeDtypeStruct((rows, 2 * tok), BF16)],
        [pltpu.VMEM((rows, tok), BF16), pltpu.VMEM((rows, LANES), F32)],
        meta,
        tokens,
    )


def stack_hidden(hidden_ref, spare_ref, out_ref, order):
    main = hidden_ref.shape[0] - spare_ref.shape[0]
    half = hidden_ref.shape[1] // 2
    core = lax.axis_index("dp")
    for at, flip in enumerate(order):
        start = pl.multiple_of((1 - core if flip else core) * half, LANES)
        out_ref[:main, at * half : (at + 1) * half] = hidden_ref[:main, pl.ds(start, half)]
        out_ref[main:, at * half : (at + 1) * half] = spare_ref[:, pl.ds(start, half)]


def out_kernel(hidden_ref, spare_ref, near_ref, far_ref, main_out, spare_out, stack_ref):
    @pl.when(pl.program_id(0) == 0)
    def _():
        stack_hidden(hidden_ref, spare_ref, stack_ref, (False, True))

    main, half = main_out.shape[0], near_ref.shape[0]
    total = dot(stack_ref[:, :half], near_ref[...]) + dot(stack_ref[:, half:], far_ref[...])
    total = total.astype(BF16)
    main_out[...] = total[:main]
    spare_out[...] = total[main:]


def project(hidden, spare_hidden, near, far, tile):
    half, width = near.shape
    slots, hid = hidden.shape
    spare = spare_hidden.shape[0]
    return call(
        out_kernel,
        width // tile,
        [whole_block(hidden.shape), whole_block(spare_hidden.shape), columns(half, tile), columns(half, tile)],
        [columns(slots - spare, tile), columns(spare, tile)],
        [jax.ShapeDtypeStruct((slots - spare, width), BF16), jax.ShapeDtypeStruct((spare, width), BF16)],
        [pltpu.VMEM((slots, hid), BF16)],
        hidden,
        spare_hidden,
        near,
        far,
    )


def give_kernel(cap, top, half, mirrored, metas_ref, main_ref, spare_ref, packed_ref, slot_ref):
    rows, slots = slot_ref.shape
    count = 2 * half
    tok = metas_ref.shape[1] // (2 * top)
    main, spare = main_ref.shape[0], spare_ref.shape[0]

    @pl.when(pl.program_id(0) == 0)
    def _():
        me = lax.axis_index("expert")
        base = lax.div(me, half) * half
        base = (lax.rem(base + half, count) if mirrored else base).astype(F32)
        mine = me.astype(F32)
        other = lax.rem(me + half, count).astype(F32)
        none = jnp.zeros((count, tok), F32)
        here, flag, clash = none, none, none
        for k in range(top):
            code = metas_ref[:, k * tok : (k + 1) * tok]
            device = jnp.floor(code * 0.5)
            here = jnp.where(device == mine, 1.0, here)
            flag = jnp.where(device == mine, code - 2.0 * device, flag)
            clash = jnp.where(device == other, 1.0, clash)
        at_spare = here * flag * (1.0 - clash)
        at_main = here - at_spare
        before = before_mask(tok)
        ones = jnp.ones((tok, LANES), BF16)
        lower = (iota((count, count), 1) < iota((count, count), 0)).astype(BF16)

        def rank(flags):
            flags = flags.astype(BF16)
            return dot(flags, before) + dot(lower, dot(flags, ones).astype(BF16))

        rank_main, rank_spare = rank(at_main), rank(at_spare)
        slot = jnp.where((at_main > 0.5) & (rank_main < main), rank_main + 1.0, none)
        slot = jnp.where((at_spare > 0.5) & (rank_spare < spare), rank_spare + (main + 1.0), slot)
        place = jnp.where(here > 0.5, dot(here.astype(BF16), before), -1.0).astype(BF16)
        group, _ = row_of(rows, cap, count)
        _, at = row_of(rows, cap, tok)
        spread = (iota((rows, count), 1) == group + base).astype(BF16)
        chosen = dot(spread, place) == at
        tens = jnp.floor(slot * (1.0 / 32.0))
        units = slot - tens * 32.0
        slot = dot(spread, tens.astype(BF16)) * 32.0 + dot(spread, units.astype(BF16))
        slot = jnp.sum(jnp.where(chosen, slot, 0.0), axis=1, keepdims=True)
        slot_ref[...] = (iota((rows, slots), 1) + 1.0 == slot).astype(BF16)

    packed = dot(slot_ref[:, :main], main_ref[...]) + dot(slot_ref[:, main:], spare_ref[...])
    packed_ref[...] = packed.astype(BF16)


def give(metas, out_main, out_spare, cap, top, half, mirrored, tile):
    main, width = out_main.shape
    spare = out_spare.shape[0]
    rows = half * cap
    return call(
        functools.partial(give_kernel, cap, top, half, mirrored),
        width // tile,
        [whole_block(metas.shape), columns(main, tile), columns(spare, tile)],
        [columns(rows, tile), whole_block((rows, main + spare))],
        [jax.ShapeDtypeStruct((rows, width), BF16), jax.ShapeDtypeStruct((rows, main + spare), BF16)],
        [],
        metas,
        out_main,
        out_spare,
    )


def mixed(mix_ref, rows_ref):
    both = dot(mix_ref[...], rows_ref[...], 0, 0)
    tok = both.shape[0] // 2
    return both[:tok] + both[tok:]


def part_kernel(mix_ref, rows_ref, part_ref):
    part_ref[...] = mixed(mix_ref, rows_ref).astype(BF16)


def total_kernel(mix_ref, rows_ref, other_ref, total_ref):
    total_ref[...] = (mixed(mix_ref, rows_ref) + other_ref[...].astype(F32)).astype(BF16)


def combine(mix, rows, other, tile):
    count, width = rows.shape
    tok = mix.shape[1] // 2
    more = [] if other is None else [other]
    return call(
        part_kernel if other is None else total_kernel,
        width // tile,
        [whole_block(mix.shape), columns(count, tile)] + [columns(tok, tile)] * len(more),
        columns(tok, tile),
        jax.ShapeDtypeStruct((tok, width), BF16),
        [],
        mix,
        rows,
        *more,
    )


def slot_kernel(own_slot, mirror_slot, own_ref, mirror_ref, main_ref, spare_ref):
    total = dot(own_slot[...], own_ref[...], 0, 0) + dot(mirror_slot[...], mirror_ref[...], 0, 0)
    total = total.astype(BF16)
    main = main_ref.shape[0]
    main_ref[...] = total[:main]
    spare_ref[...] = total[main:]


def to_slots(own_slot, mirror_slot, own, mirror, main, tile):
    rows, width = own.shape
    slots = own_slot.shape[1]
    return call(
        slot_kernel,
        width // tile,
        [whole_block(own_slot.shape), whole_block(own_slot.shape), columns(rows, tile), columns(rows, tile)],
        [columns(main, tile), columns(slots - main, tile)],
        [jax.ShapeDtypeStruct((main, width), BF16), jax.ShapeDtypeStruct((slots - main, width), BF16)],
        [],
        own_slot,
        mirror_slot,
        own,
        mirror,
    )


def weight_kernel(flip, with_other, hidden_ref, spare_ref, main_ref, grad_ref, *rest):
    out_ref, stack_ref, grads_ref = rest[-3:]
    main = main_ref.shape[0]

    @pl.when(pl.program_id(0) == 0)
    def _():
        stack_hidden(hidden_ref, spare_ref, stack_ref, (flip,))

    grads_ref[:main] = main_ref[...]
    grads_ref[main:] = grad_ref[...]
    total = dot(stack_ref[...], grads_ref[...], 0, 0)
    if with_other:
        total = total + rest[0][...].astype(F32)
    out_ref[...] = total.astype(BF16)


def weight_part(hidden, spare_hidden, grads_main, grads_spare, other, flip, tile):
    slots, hid = hidden.shape
    main, width = grads_main.shape
    spare = slots - main
    more = [] if other is None else [other]
    return call(
        functools.partial(weight_kernel, flip, bool(more)),
        width // tile,
        [whole_block(hidden.shape), whole_block(spare_hidden.shape), columns(main, tile), columns(spare, tile)]
        + [columns(hid // 2, tile)] * len(more),
        columns(hid // 2, tile),
        jax.ShapeDtypeStruct((hid // 2, width), BF16),
        [pltpu.VMEM((slots, hid // 2), BF16), pltpu.VMEM((slots, tile), BF16)],
        hidden,
        spare_hidden,
        grads_main,
        grads_spare,
        *more,
    )


def back_kernel(main_ref, spare_ref, near_ref, far_ref, main_out, spare_out, sum_ref):
    step = pl.program_id(0)
    core = lax.axis_index("dp")
    half = near_ref.shape[0]

    @pl.when(step == 0)
    def _():
        sum_ref[...] = jnp.zeros_like(sum_ref)

    main = main_ref.shape[0]
    for at, weight in ((0, near_ref), (half, far_ref)):
        sum_ref[:main, at : at + half] += dot(main_ref[...], weight[...], 1, 1)
        sum_ref[main:, at : at + half] += dot(spare_ref[...], weight[...], 1, 1)

    @pl.when(step == pl.num_programs(0) - 1)
    def _():
        near = pl.multiple_of(core * half, LANES)
        far = pl.multiple_of((1 - core) * half, LANES)
        for start, at in ((near, 0), (far, half)):
            total = sum_ref[:, at : at + half].astype(BF16)
            main_out[:, pl.ds(start, half)] = total[:main]
            spare_out[:, pl.ds(start, half)] = total[main:]


def project_back(grads_main, grads_spare, near, far, tile):
    main, width = grads_main.shape
    spare = grads_spare.shape[0]
    half = near.shape[0]
    return call(
        back_kernel,
        width // tile,
        [columns(main, tile), columns(spare, tile), columns(half, tile), columns(half, tile)],
        [whole_block((main, 2 * half)), whole_block((spare, 2 * half))],
        [jax.ShapeDtypeStruct((main, 2 * half), BF16), jax.ShapeDtypeStruct((spare, 2 * half), BF16)],
        [pltpu.VMEM((main + spare, 2 * half), F32)],
        grads_main,
        grads_spare,
        near,
        far,
    )


def local(hidden_saved, down_weight, route_device, replica_flag, gate_values, grad_out):
    count = lax.axis_size("expert")
    half = count // 2
    tok, top = route_device.shape
    width = grad_out.shape[1]
    cap = 5 * tok * top // (4 * count)
    main = 3 * tok * top // 4
    hidden = hidden_saved[0, 0]
    near = down_weight[0]
    tile = width // 4
    groups = [list(range(half)), list(range(half, count))]

    def to_half(rows):
        return lax.all_to_all(
            rows.reshape(half, cap, width), "expert", 0, 0, axis_index_groups=groups, tiled=True
        ).reshape(half * cap, width)

    mirror_grad = swapped(grad_out, "expert", half)
    far = swapped(near, "dp", 1)
    spare_hidden = swapped(hidden[main:], "expert", half)
    codes = (route_device * 2 + replica_flag).T.reshape(1, tok * top).astype(F32)
    meta = jnp.concatenate([codes, gate_values.T.reshape(1, tok * top)], axis=1)
    metas = lax.all_to_all(
        jnp.broadcast_to(meta, (count, 2 * tok * top)), "expert", 0, 0, tiled=True
    )

    packed_own, mix_own = pack(meta, grad_out, cap, top, half, False, tile)
    arrived_own = to_half(packed_own)
    out_main, out_spare = project(hidden, spare_hidden, near, far, tile)
    out_spare = swapped(out_spare, "expert", half)
    packed_mirror, mix_mirror = pack(metas, mirror_grad, cap, top, half, True, tile)
    arrived_mirror = to_half(packed_mirror)
    given_mirror, slot_mirror = give(metas, out_main, out_spare, cap, top, half, True, tile)
    returned_mirror = to_half(given_mirror)
    given_own, slot_own = give(metas, out_main, out_spare, cap, top, half, False, tile)
    returned_own = to_half(given_own)
    grads_main, grads_spare = to_slots(slot_own, slot_mirror, arrived_own, arrived_mirror, main, tile)
    grads_spare = swapped(grads_spare, "expert", half)
    part = combine(mix_mirror, returned_mirror, None, tile)
    part = swapped(part, "expert", half)
    far_part = weight_part(hidden, spare_hidden, grads_main, grads_spare, None, True, tile)
    far_part = swapped(far_part, "dp", 1)
    back_main, back_spare = project_back(grads_main, grads_spare, near, far, tile)
    back_spare = swapped(back_spare, "expert", half)
    layer_out = combine(mix_own, returned_own, part, tile)
    grad_weight = weight_part(hidden, spare_hidden, grads_main, grads_spare, far_part, False, tile)
    grad_hidden = jnp.concatenate([back_main, back_spare], axis=0)
    return (layer_out, grad_hidden[None, None], grad_weight[None])


def solution(mesh):
    in_specs = (
        P("dp", "expert", None, None),
        P("expert", "dp", None),
        P(("dp", "expert"), None),
        P(("dp", "expert"), None),
        P(("dp", "expert"), None),
        P(("dp", "expert"), None),
    )
    out_specs = (P(("dp", "expert"), None), P("dp", "expert", None, None), P("expert", "dp", None))
    return jax.shard_map(local, mesh=mesh, in_specs=in_specs, out_specs=out_specs, check_vma=False)
```

profile of v0, /device:TPU:0, one launch (start us, length us, event | category | flops | bytes accessed | tf_op | source)
XLA Modules:
  0.0 257.8 jit_solution(10808840458726626426)
XLA Ops:
  0.6 0.7 add_convert_fusion
  1.3 0.7 pad_maximum_fusion.meta_ref
  2.0 0.7 broadcast_in_dim.11
  2.7 8.3 %all-to-all-start = ((f32[16,1,1024]{2,1,0:T(1,128)}), f32[16,1,1024]{2,1,0:T(1,128)S(1)}, u32[]{:S(2)}, u32[]{:S(2)}) async-start(f32[16,1,1024]{2,1,0:T(1,128)} %broadcast_in_dim.11), calls=%async_computation | async-start | bytes 131072 | tf_op jit(solution)/shard_map/all_to_all | solution.py:378
  11.0 0.0 copy-start.10
  11.0 1.2 copy-done.10
  12.2 2.0 shard_map.85
  14.2 0.0 copy-start.8
  14.2 1.4 copy-done.8
  15.6 0.7 copy-done.14
  16.2 2.3 all-to-all-done
  18.5 3.7 %all-to-all-start.3 = ((bf16[8,40,3584]{2,1,0:T(8,128)(2,1)}), bf16[8,40,3584]{2,1,0:T(8,128)(2,1)S(1)}, u32[]{:S(2)}, u32[]{:S(2)}) async-start(bf16[8,40,3584]{2,1,0:T(8,128)(2,1)} %bitcast.34), calls=%async_computation.3 | async-start | bytes 4587520 | tf_op jit(solution)/shard_map/all_to_all | solution.py:369
  22.3 0.0 copy-done.11
  22.3 1.5 collective-permute-start.3
  23.8 0.0 collective-permute-start.1
  23.8 41.8 %collective-permute-done.3.tokens_ref = bf16[128,3584]{1,0:T(8,128)(2,1)S(1)} collective-permute-done((bf16[128,3584]{1,0:T(8,128)(2,1)S(1)}, bf16[128,3584]{1,0:T(8,128)(2,1)S(1)}, u32[]{:S(2)}, u32[]{:S(2)}) %collective-permute-start.3) | collective-permute-done | bytes 917536 | tf_op jit(solution)/shard_map/ppermute | solution.py:17
  65.6 2.0 shard_map.88
  67.6 0.0 copy-start.7
  67.6 1.4 copy-done.7
  69.0 0.0 all-to-all-done.3
  69.0 0.7 copy-done.16
  69.7 0.9 copy-done.2
  70.6 9.3 %all-to-all-start.4 = ((bf16[8,40,3584]{2,1,0:T(8,128)(2,1)}), bf16[8,40,3584]{2,1,0:T(8,128)(2,1)}, u32[]{:S(2)}, u32[]{:S(2)}) async-start(bf16[8,40,3584]{2,1,0:T(8,128)(2,1)} %bitcast.33), calls=%async_computation.4 | async-start | bytes 4587520 | tf_op jit(solution)/shard_map/all_to_all | solution.py:369
  79.8 0.9 slice_bitcast_fusion
  80.7 0.1 collective-permute-start
  80.8 24.9 %collective-permute-done.spare_ref = bf16[64,1024]{1,0:T(8,128)(2,1)S(1)} collective-permute-done((bf16[64,1024]{1,0:T(8,128)(2,1)S(1)}, bf16[64,1024]{1,0:T(8,128)(2,1)S(1)}, u32[]{:S(2)}, u32[]{:S(2)}) %collective-permute-start) | collective-permute-done | bytes 131104 | tf_op jit(solution)/shard_map/ppermute | solution.py:17
  105.7 0.0 collective-permute-done.1.far_ref
  105.7 2.0 copy-done
  107.8 1.2 copy-done.4
  109.0 6.2 %shard_map.86 = (bf16[384,3584]{1,0:T(8,128)(2,1)S(1)}, bf16[64,3584]{1,0:T(8,128)(2,1)S(1)}) custom-call(bf16[448,1024]{1,0:T(8,128)(2,1)S(1)} %bitcast.29, bf16[64,1024]{1,0:T(8,128)(2,1)S(1)} %collective-permute-done.spare_ref, bf16[512,3584]{1,0:T(8,128)(2,1)S(1)} %bitcast.26, bf16[512,3584]{1,0:T(8,128)(2,1)} %collective-permute-done.1.far_ref), custom_call_target="tpu_custom_call" | custom-call | tf_op jit(solution)/shard_map/pallas_call | solution.py:40
  115.1 3.4 %collective-permute-start.2 = (bf16[64,3584]{1,0:T(8,128)(2,1)S(1)}, bf16[64,3584]{1,0:T(8,128)(2,1)S(1)}, u32[]{:S(2)}, u32[]{:S(2)}) collective-permute-start(bf16[64,3584]{1,0:T(8,128)(2,1)S(1)} %get-tuple-element.19), channel_id=1, source_target_pairs={{0,8},{1,9},{2,10},{3,11},{4,12},{5,13},{6,14},{7,15},{8,0},{9,1},... | collective-permute-start | bytes 1376264 | tf_op jit(solution)/shard_map/ppermute | solution.py:17
  118.6 17.7 %collective-permute-done.2.spare_ref = bf16[64,3584]{1,0:T(8,128)(2,1)S(1)} collective-permute-done((bf16[64,3584]{1,0:T(8,128)(2,1)S(1)}, bf16[64,3584]{1,0:T(8,128)(2,1)S(1)}, u32[]{:S(2)}, u32[]{:S(2)}) %collective-permute-start.2) | collective-permute-done | bytes 458784 | tf_op jit(solution)/shard_map/ppermute | solution.py:17
  136.3 3.5 %shard_map.89 = (bf16[320,3584]{1,0:T(8,128)(2,1)S(1)}, bf16[320,448]{1,0:T(8,128)(2,1)S(1)}) custom-call(f32[16,1024]{1,0:T(8,128)S(1)} %bitcast.37, bf16[384,3584]{1,0:T(8,128)(2,1)S(1)} %get-tuple-element.18.main_ref, bf16[64,3584]{1,0:T(8,128)(2,1)S(1)} %collective-permute-done.2.spare_ref), custom_call_target="tpu_custom_call" | custom-call | tf_op jit(solution)/shard_map/pallas_call | solution.py:40
  139.8 0.0 copy-start.9
  139.8 1.4 copy-done.9
  141.1 0.7 copy-done.12
  141.9 0.0 all-to-all-done.4
  141.9 4.4 %all-to-all-start.2 = ((bf16[8,40,3584]{2,1,0:T(8,128)(2,1)}), bf16[8,40,3584]{2,1,0:T(8,128)(2,1)}, u32[]{:S(2)}, u32[]{:S(2)}) async-start(bf16[8,40,3584]{2,1,0:T(8,128)(2,1)} %bitcast.35), calls=%async_computation.2 | async-start | bytes 4587520 | tf_op jit(solution)/shard_map/all_to_all | solution.py:369
  146.3 0.0 copy-start.3
  146.3 0.0 copy-start.13
  146.3 3.5 %shard_map.87 = (bf16[320,3584]{1,0:T(8,128)(2,1)S(1)}, bf16[320,448]{1,0:T(8,128)(2,1)S(1)}) custom-call(f32[16,1024]{1,0:T(8,128)S(1)} %bitcast.38, bf16[384,3584]{1,0:T(8,128)(2,1)S(1)} %get-tuple-element.18.main_ref, bf16[64,3584]{1,0:T(8,128)(2,1)S(1)} %collective-permute-done.2.spare_ref), custom_call_target="tpu_custom_call" | custom-call | tf_op jit(solution)/shard_map/pallas_call | solution.py:40
  149.8 0.0 copy-start.6
  149.8 1.4 copy-done.6
  151.2 0.0 copy-done.13
  151.2 6.5 %shard_map.92 = (bf16[384,3584]{1,0:T(8,128)(2,1)S(1)}, bf16[64,3584]{1,0:T(8,128)(2,1)}) custom-call(bf16[320,448]{1,0:T(8,128)(2,1)S(1)} %get-tuple-element.23.own_slot, bf16[320,448]{1,0:T(8,128)(2,1)S(1)} %copy-done.13, bf16[320,3584]{1,0:T(8,128)(2,1)S(1)} %bitcast.28, bf16[320,3584]{1,0:T(8,128)(2,1)} %bitcast.15.mirror_ref), custom_call_target="tpu_custom_call" | custom-call | tf_op jit(solution)/shard_map/pallas_call | solution.py:40
  157.7 0.0 collective-permute-start.5
  157.7 25.4 %all-to-all-done.2 = bf16[8,40,3584]{2,1,0:T(8,128)(2,1)} async-done(((bf16[8,40,3584]{2,1,0:T(8,128)(2,1)}), bf16[8,40,3584]{2,1,0:T(8,128)(2,1)}, u32[]{:S(2)}, u32[]{:S(2)}) %all-to-all-start.2) | async-done | bytes 2293792 | tf_op jit(solution)/shard_map/all_to_all | solution.py:369
  183.1 6.0 %all-to-all-start.1 = ((bf16[8,40,3584]{2,1,0:T(8,128)(2,1)}), bf16[8,40,3584]{2,1,0:T(8,128)(2,1)}, u32[]{:S(2)}, u32[]{:S(2)}) async-start(bf16[8,40,3584]{2,1,0:T(8,128)(2,1)} %bitcast.32), calls=%async_computation.1 | async-start | bytes 4587520 | tf_op jit(solution)/shard_map/all_to_all | solution.py:369
  189.1 0.0 collective-permute-done.5.spare_ref.grad_ref
  189.1 0.0 copy-start.5
  189.1 1.2 copy-done.5
  190.3 3.6 %shard_map.94 = bf16[512,3584]{1,0:T(8,128)(2,1)S(1)} custom-call(bf16[448,1024]{1,0:T(8,128)(2,1)S(1)} %bitcast.30, bf16[64,1024]{1,0:T(8,128)(2,1)S(1)} %collective-permute-done.spare_ref, bf16[384,3584]{1,0:T(8,128)(2,1)S(1)} %get-tuple-element.27.main_ref, bf16[64,3584]{1,0:T(8,128)(2,1)S(1)} %collective-permute-done.5.spare_ref.grad_ref), custom_call_target="tpu_custom_call" | custom-call | tf_op jit(solution)/shard_map/pallas_call | solution.py:40
  193.9 0.1 collective-permute-start.7
  194.0 4.5 %shard_map.90 = bf16[128,3584]{1,0:T(8,128)(2,1)} custom-call(bf16[320,256]{1,0:T(8,128)(2,1)S(1)} %copy-done.17, bf16[320,3584]{1,0:T(8,128)(2,1)} %bitcast.11.rows_ref), custom_call_target="tpu_custom_call" | custom-call | tf_op jit(solution)/shard_map/pallas_call | solution.py:40
  198.4 0.1 collective-permute-start.4
  198.5 8.0 %shard_map.93 = (bf16[384,1024]{1,0:T(8,128)(2,1)S(1)}, bf16[64,1024]{1,0:T(8,128)(2,1)S(1)}) custom-call(bf16[384,3584]{1,0:T(8,128)(2,1)S(1)} %get-tuple-element.27.main_ref, bf16[64,3584]{1,0:T(8,128)(2,1)S(1)} %collective-permute-done.5.spare_ref.grad_ref, bf16[512,3584]{1,0:T(8,128)(2,1)S(1)} %bitcast.27, bf16[512,3584]{1,0:T(8,128)(2,1)} %collective-permute-done.1.far_ref), custom_call_target="tpu_custom_call" | custom-call | tf_op jit(solution)/shard_map/pallas_call | solution.py:40
  206.5 2.9 %collective-permute-start.6 = (bf16[64,1024]{1,0:T(8,128)(2,1)S(1)}, bf16[64,1024]{1,0:T(8,128)(2,1)S(1)}, u32[]{:S(2)}, u32[]{:S(2)}) collective-permute-start(bf16[64,1024]{1,0:T(8,128)(2,1)S(1)} %get-tuple-element.30), channel_id=1, source_target_pairs={{0,8},{1,9},{2,10},{3,11},{4,12},{5,13},{6,14},{7,15},{8,0},{9,1},... | collective-permute-start | bytes 393224 | tf_op jit(solution)/shard_map/ppermute | solution.py:17
  209.4 38.2 %collective-permute-done.6 = bf16[64,1024]{1,0:T(8,128)(2,1)S(1)} collective-permute-done((bf16[64,1024]{1,0:T(8,128)(2,1)S(1)}, bf16[64,1024]{1,0:T(8,128)(2,1)S(1)}, u32[]{:S(2)}, u32[]{:S(2)}) %collective-permute-start.6) | collective-permute-done | bytes 131104 | tf_op jit(solution)/shard_map/ppermute | solution.py:17
  247.6 1.0 maximum_bitcast_fusion
  248.6 0.0 collective-permute-done.7.rest_0_
  248.6 4.6 %shard_map.95 = bf16[512,3584]{1,0:T(8,128)(2,1)} custom-call(bf16[448,1024]{1,0:T(8,128)(2,1)S(1)} %bitcast.31, bf16[64,1024]{1,0:T(8,128)(2,1)S(1)} %collective-permute-done.spare_ref, bf16[384,3584]{1,0:T(8,128)(2,1)S(1)} %get-tuple-element.27.main_ref, bf16[64,3584]{1,0:T(8,128)(2,1)S(1)} %collective-permute-done.5.spare_ref.grad_ref, ...), custom_call_target="tpu_custom_call" | custom-call | tf_op jit(solution)/shard_map/pallas_call | solution.py:40
  253.2 0.0 all-to-all-done.1
  253.2 0.0 collective-permute-done.4.other_ref
  253.2 4.6 %shard_map.91 = bf16[128,3584]{1,0:T(8,128)(2,1)} custom-call(bf16[320,256]{1,0:T(8,128)(2,1)S(1)} %copy-done.15, bf16[320,3584]{1,0:T(8,128)(2,1)} %bitcast.9.rows_ref, bf16[128,3584]{1,0:T(8,128)(2,1)} %collective-permute-done.4.other_ref), custom_call_target="tpu_custom_call" | custom-call | tf_op jit(solution)/shard_map/pallas_call | solution.py:40
  (15 shorter events, 0.0 us)
Async XLA Ops:
  2.7 15.9 %all-to-all-start = ((f32[16,1,1024]{2,1,0:T(1,128)}), f32[16,1,1024]{2,1,0:T(1,128)S(1)}, u32[]{:S(2)}, u32[]{:S(2)}) async-start(f32[16,1,1024]{2,1,0:T(1,128)} %broadcast_in_dim.11), calls=%async_computation | async-start | bytes 131072 | tf_op jit(solution)/shard_map/all_to_all | solution.py:378
  11.0 1.2 copy-start.10
  14.2 1.4 copy-start.8
  15.6 0.7 copy-start.14
  18.5 3.8 %copy-start.11 = (bf16[128,3584]{1,0:T(8,128)(2,1)S(1)}, bf16[128,3584]{1,0:T(8,128)(2,1)}, u32[]{:S(2)}) copy-start(bf16[128,3584]{1,0:T(8,128)(2,1)} %tokens_ref.1) | copy-start | bytes 2752516
  18.5 50.5 %all-to-all-start.3 = ((bf16[8,40,3584]{2,1,0:T(8,128)(2,1)}), bf16[8,40,3584]{2,1,0:T(8,128)(2,1)S(1)}, u32[]{:S(2)}, u32[]{:S(2)}) async-start(bf16[8,40,3584]{2,1,0:T(8,128)(2,1)} %bitcast.34), calls=%async_computation.3 | async-start | bytes 4587520 | tf_op jit(solution)/shard_map/all_to_all | solution.py:369
  22.3 43.3 %collective-permute-start.3 = (bf16[128,3584]{1,0:T(8,128)(2,1)S(1)}, bf16[128,3584]{1,0:T(8,128)(2,1)S(1)}, u32[]{:S(2)}, u32[]{:S(2)}) collective-permute-start(bf16[128,3584]{1,0:T(8,128)(2,1)S(1)} %copy-done.11), channel_id=1, source_target_pairs={{0,8},{1,9},{2,10},{3,11},{4,12},{5,13},{6,14},{7,15},{8,0},{9,1},... | collective-permute-start | bytes 2752520 | tf_op jit(solution)/shard_map/ppermute | solution.py:17
  23.8 81.9 %collective-permute-start.1 = (bf16[512,3584]{1,0:T(8,128)(2,1)}, bf16[512,3584]{1,0:T(8,128)(2,1)}, u32[]{:S(2)}, u32[]{:S(2)}) collective-permute-start(bf16[512,3584]{1,0:T(8,128)(2,1)} %bitcast.25), channel_id=1, source_target_pairs={{0,16},{16,0},{1,17},{17,1},{2,18},{18,2},{3,19},{19,3},{4,20},{20... | collective-permute-start | bytes 11010056 | tf_op jit(solution)/shard_map/ppermute | solution.py:17
  67.6 1.4 copy-start.7
  69.0 0.7 copy-start.16
  69.0 1.5 copy-start.2
  70.6 71.3 %all-to-all-start.4 = ((bf16[8,40,3584]{2,1,0:T(8,128)(2,1)}), bf16[8,40,3584]{2,1,0:T(8,128)(2,1)}, u32[]{:S(2)}, u32[]{:S(2)}) async-start(bf16[8,40,3584]{2,1,0:T(8,128)(2,1)} %bitcast.33), calls=%async_computation.4 | async-start | bytes 4587520 | tf_op jit(solution)/shard_map/all_to_all | solution.py:369
  80.7 25.0 %collective-permute-start = (bf16[64,1024]{1,0:T(8,128)(2,1)S(1)}, bf16[64,1024]{1,0:T(8,128)(2,1)S(1)}, u32[]{:S(2)}, u32[]{:S(2)}) collective-permute-start(bf16[64,1024]{1,0:T(8,128)(2,1)S(1)} %slice_bitcast_fusion), channel_id=1, source_target_pairs={{0,8},{1,9},{2,10},{3,11},{4,12},{5,13},{6,14},{7,15},{8,0},{9,1},... | collective-permute-start | bytes 393224 | tf_op jit(solution)/shard_map/ppermute | solution.py:17
  105.7 2.0 copy-start
  107.8 1.2 copy-start.4
  115.1 21.1 %collective-permute-start.2 = (bf16[64,3584]{1,0:T(8,128)(2,1)S(1)}, bf16[64,3584]{1,0:T(8,128)(2,1)S(1)}, u32[]{:S(2)}, u32[]{:S(2)}) collective-permute-start(bf16[64,3584]{1,0:T(8,128)(2,1)S(1)} %get-tuple-element.19), channel_id=1, source_target_pairs={{0,8},{1,9},{2,10},{3,11},{4,12},{5,13},{6,14},{7,15},{8,0},{9,1},... | collective-permute-start | bytes 1376264 | tf_op jit(solution)/shard_map/ppermute | solution.py:17
  139.8 1.4 copy-start.9
  141.1 0.7 copy-start.12
  141.9 41.3 %all-to-all-start.2 = ((bf16[8,40,3584]{2,1,0:T(8,128)(2,1)}), bf16[8,40,3584]{2,1,0:T(8,128)(2,1)}, u32[]{:S(2)}, u32[]{:S(2)}) async-start(bf16[8,40,3584]{2,1,0:T(8,128)(2,1)} %bitcast.35), calls=%async_computation.2 | async-start | bytes 4587520 | tf_op jit(solution)/shard_map/all_to_all | solution.py:369
  146.3 4.9 %copy-start.3 = (bf16[8,40,3584]{2,1,0:T(8,128)(2,1)S(1)}, bf16[8,40,3584]{2,1,0:T(8,128)(2,1)}, u32[]{:S(2)}) copy-start(bf16[8,40,3584]{2,1,0:T(8,128)(2,1)} %copy-done.2) | copy-start | bytes 6881284
  146.3 4.9 %copy-start.13 = (bf16[320,448]{1,0:T(8,128)(2,1)S(1)}, bf16[320,448]{1,0:T(8,128)(2,1)}, u32[]{:S(2)}) copy-start(bf16[320,448]{1,0:T(8,128)(2,1)} %copy-done.12) | copy-start | bytes 860164
  149.8 1.4 copy-start.6
  157.7 31.4 %collective-permute-start.5 = (bf16[64,3584]{1,0:T(8,128)(2,1)}, bf16[64,3584]{1,0:T(8,128)(2,1)S(1)}, u32[]{:S(2)}, u32[]{:S(2)}) collective-permute-start(bf16[64,3584]{1,0:T(8,128)(2,1)} %get-tuple-element.28), channel_id=1, source_target_pairs={{0,8},{1,9},{2,10},{3,11},{4,12},{5,13},{6,14},{7,15},{8,0},{9,1},... | collective-permute-start | bytes 1376264 | tf_op jit(solution)/shard_map/ppermute | solution.py:17
  183.1 70.1 %all-to-all-start.1 = ((bf16[8,40,3584]{2,1,0:T(8,128)(2,1)}), bf16[8,40,3584]{2,1,0:T(8,128)(2,1)}, u32[]{:S(2)}, u32[]{:S(2)}) async-start(bf16[8,40,3584]{2,1,0:T(8,128)(2,1)} %bitcast.32), calls=%async_computation.1 | async-start | bytes 4587520 | tf_op jit(solution)/shard_map/all_to_all | solution.py:369
  189.1 1.2 copy-start.5
  190.3 3.7 %copy-start.17 = (bf16[320,256]{1,0:T(8,128)(2,1)S(1)}, bf16[320,256]{1,0:T(8,128)(2,1)}, u32[]{:S(2)}) copy-start(bf16[320,256]{1,0:T(8,128)(2,1)} %copy-done.16) | copy-start | bytes 491524
  190.3 8.2 %copy-start.1 = (bf16[1,512,3584]{2,1,0:T(8,128)(2,1)S(1)}, bf16[1,512,3584]{2,1,0:T(8,128)(2,1)}, u32[]{:S(2)}) copy-start(bf16[1,512,3584]{2,1,0:T(8,128)(2,1)} %param.7) | copy-start | bytes 11010052
  193.9 54.7 %collective-permute-start.7 = (bf16[512,3584]{1,0:T(8,128)(2,1)S(1)}, bf16[512,3584]{1,0:T(8,128)(2,1)S(1)}, u32[]{:S(2)}, u32[]{:S(2)}) collective-permute-start(bf16[512,3584]{1,0:T(8,128)(2,1)S(1)} %shard_map.94), channel_id=1, source_target_pairs={{0,16},{16,0},{1,17},{17,1},{2,18},{18,2},{3,19},{19,3},{4,20},{20... | collective-permute-start | bytes 11010056 | tf_op jit(solution)/shard_map/ppermute | solution.py:17
  198.4 54.8 %collective-permute-start.4 = (bf16[128,3584]{1,0:T(8,128)(2,1)}, bf16[128,3584]{1,0:T(8,128)(2,1)}, u32[]{:S(2)}, u32[]{:S(2)}) collective-permute-start(bf16[128,3584]{1,0:T(8,128)(2,1)} %shard_map.90), channel_id=1, source_target_pairs={{0,8},{1,9},{2,10},{3,11},{4,12},{5,13},{6,14},{7,15},{8,0},{9,1},... | collective-permute-start | bytes 2752520 | tf_op jit(solution)/shard_map/ppermute | solution.py:17
  206.5 41.1 %collective-permute-start.6 = (bf16[64,1024]{1,0:T(8,128)(2,1)S(1)}, bf16[64,1024]{1,0:T(8,128)(2,1)S(1)}, u32[]{:S(2)}, u32[]{:S(2)}) collective-permute-start(bf16[64,1024]{1,0:T(8,128)(2,1)S(1)} %get-tuple-element.30), channel_id=1, source_target_pairs={{0,8},{1,9},{2,10},{3,11},{4,12},{5,13},{6,14},{7,15},{8,0},{9,1},... | collective-permute-start | bytes 393224 | tf_op jit(solution)/shard_map/ppermute | solution.py:17
  248.6 4.6 %copy-start.15 = (bf16[320,256]{1,0:T(8,128)(2,1)S(1)}, bf16[320,256]{1,0:T(8,128)(2,1)}, u32[]{:S(2)}) copy-start(bf16[320,256]{1,0:T(8,128)(2,1)} %copy-done.14) | copy-start | bytes 491524
where the time goes:
time: 259 us; the launch traced here: 258 us
  waiting for transfers between devices  150 us (58%)
  Pallas kernels  48.9 us (19%)
  starting transfers between devices  39.7 us (15%)
  local copies, waits for them, and re-layouts  15.6 us (6%)
    ppermute x8, waiting for transfers between devices, swapped(): return lax.ppermute(value, axis, pairs)  123 us
    pallas_call x11, Pallas kernels, call(): pl.pallas_call(body, grid=(grid,), in_specs=in_specs, out_specs=out_specs...  48.9 us
    all_to_all x4, waiting for transfers between devices, to_half(): lax.all_to_all(rows.reshape(half, cap, width), 'expert', 0, 0, axis_index...  25.5 us
    all_to_all x4, starting transfers between devices, to_half(): lax.all_to_all(rows.reshape(half, cap, width), 'expert', 0, 0, axis_index...  23.4 us
    unnamed x37, local copies, waits for them, and re-layouts  14.1 us
    all_to_all x1, starting transfers between devices, local(): lax.all_to_all(jnp.broadcast_to(meta, (count, 2 * tok * top)), 'expert',...  8.31 us
    ppermute x8, starting transfers between devices, swapped(): return lax.ppermute(value, axis, pairs)  8.07 us
  transfers between devices with their start and end apart: 13, of which 6 were waited for; matrix products, arithmetic and copies ran while one was open for 1% of the time, Pallas kernels for 17%

commit v1 on v0

v1 whole, which is shorter than its diff:
```python
import functools
import jax
import jax.numpy as jnp
from jax import lax
from jax.experimental import pallas as pl
from jax.experimental.pallas import tpu as pltpu
from jax.sharding import PartitionSpec as P

F32, BF16, I32 = jnp.float32, jnp.bfloat16, jnp.int32
LANES = 128
LONG = 400_000_000
VMEM_LIMIT = 60 * 1024 * 1024


def swapped(value, axis, distance):
    count = lax.axis_size(axis)
    pairs = [(source, (source + distance) % count) for source in range(count)]
    return lax.ppermute(value, axis, pairs)


def dot(left, right, left_dim=1, right_dim=0):
    contract = (((left_dim,), (right_dim,)), ((), ()))
    return lax.dot_general(left, right, contract, preferred_element_type=F32)


def iota(shape, dim):
    return lax.broadcasted_iota(I32, shape, dim).astype(F32)


def row_of(rows, cap, lanes):
    row = iota((rows, lanes), 0)
    group = jnp.floor((row + 0.5) * (1.0 / cap))
    return group, row - group * cap


def before_mask(size):
    return (iota((size, size), 0) < iota((size, size), 1)).astype(BF16)


def call(body, grid, in_specs, out_specs, out_shape, scratch, *operands, cost=0):
    return pl.pallas_call(
        body,
        grid=(grid,),
        in_specs=in_specs,
        out_specs=out_specs,
        out_shape=out_shape,
        scratch_shapes=scratch,
        compiler_params=pltpu.CompilerParams(vmem_limit_bytes=VMEM_LIMIT),
        cost_estimate=pl.CostEstimate(flops=0, bytes_accessed=cost, transcendentals=0),
    )(*operands)


def anywhere():
    return pl.BlockSpec(memory_space=pl.ANY)


def whole_block(shape):
    return pl.BlockSpec(shape, lambda step: (0,) * len(shape))


def columns(rows, tile):
    return pl.BlockSpec((rows, tile), lambda step: (0, step))


def head_kernel(device_ref, flag_ref, gate_ref, tokens_ref, hidden_ref, payload_ref, spare_ref):
    top, tok = device_ref.shape
    width = tokens_ref.shape[1]
    gate = gate_ref[...]
    high = gate.astype(BF16).astype(F32)
    mid = (gate - high).astype(BF16).astype(F32)
    low = gate - high - mid
    parts = [device_ref[...].astype(F32), flag_ref[...].astype(F32), high, mid, low]
    filler = jnp.zeros((LANES - len(parts) * top, tok), F32)
    payload_ref[:, :width] = tokens_ref[...]
    payload_ref[:, width:] = jnp.concatenate(parts + [filler], axis=0).T.astype(BF16)
    spare_ref[...] = hidden_ref[...]


def head(devices, flags, gates, tokens, hidden, spare):
    top = devices.shape[0]
    tok, width = tokens.shape
    slots, hid = hidden.shape
    return call(
        head_kernel,
        1,
        [whole_block((top, tok))] * 3
        + [whole_block((tok, width)), pl.BlockSpec((spare, hid), lambda step: (slots // spare - 1, 0))],
        [whole_block((tok, width + LANES)), whole_block((spare, hid))],
        [jax.ShapeDtypeStruct((tok, width + LANES), BF16), jax.ShapeDtypeStruct((spare, hid), BF16)],
        [],
        devices,
        flags,
        gates,
        tokens,
        hidden,
    )


def pack_kernel(cap, top, half, tiles, meta_ref, tokens_ref, *rest):
    packed_ref, mix_ref, sel_ref, gate_ref, kind_ref = rest[-5:]
    rows, tok = sel_ref.shape
    step = pl.program_id(0)

    @pl.when(step == 0)
    def _():
        me = lax.axis_index("expert")
        first = (lax.div(me, half) * half).astype(F32)
        meta = meta_ref[...].astype(F32).T
        part = lambda which, k: meta[which * top + k : which * top + k + 1]
        devices = [part(0, k) for k in range(top)]
        dest = iota((LANES, tok), 0)
        inside = dest < half
        dest = dest + first
        none = jnp.zeros((LANES, tok), F32)
        hit, spare, high, mid, low = none, none, none, none, none
        for k in range(top):
            partner = devices[k] + jnp.where(devices[k] < half, 1.0 * half, -1.0 * half)
            wants = part(1, k)
            for other in devices:
                wants = jnp.where(other == partner, 0.0, wants)
            named = (dest == devices[k]) & inside
            hit = jnp.where(named, 1.0, hit)
            spare = jnp.where(named, wants, spare)
            high = jnp.where(named, part(2, k), high)
            mid = jnp.where(named, part(3, k), mid)
            low = jnp.where(named, part(4, k), low)
        place = dot(hit.astype(BF16), before_mask(tok))
        place = jnp.where(hit > 0.5, place, -1.0)
        group, at = row_of(rows, cap, LANES)
        spread = (iota((rows, LANES), 1) == group).astype(BF16)
        to_rows = lambda table: dot(spread, table.astype(BF16))
        chosen = to_rows(place) == at
        of_row = lambda table: jnp.sum(jnp.where(chosen, table, 0.0), axis=1, keepdims=True)
        high, mid, low = to_rows(high), to_rows(mid), to_rows(low)
        sel = jnp.where(chosen, 1.0, jnp.zeros((rows, tok), F32))
        sel_ref[...] = sel.astype(BF16)
        gate_ref[...] = jnp.broadcast_to(of_row(high + mid + low), (rows, LANES))
        mix_ref[:tok] = (sel * high).T.astype(BF16)
        mix_ref[tok:] = (sel * mid).T.astype(BF16)
        is_spare = of_row(to_rows(spare))
        is_main = of_row(sel) - is_spare
        lane = iota((rows, LANES), 1)
        kind = jnp.where(lane == 0.0, is_main, jnp.where(lane == 1.0, is_spare, 0.0))
        kind_ref[...] = kind.astype(BF16)

    @pl.when(step < tiles)
    def _():
        packed = dot(sel_ref[...], tokens_ref[...]) * gate_ref[:, :1]
        packed_ref[...] = packed.astype(BF16)

    @pl.when(step == tiles)
    def _():
        packed_ref[:, :LANES] = kind_ref[...]


def pack(payload, cap, top, half, tile, cost, *after):
    tok, wide = payload.shape
    rows = half * cap
    tiles = (wide - LANES) // tile
    return call(
        functools.partial(pack_kernel, cap, top, half, tiles),
        tiles + 1,
        [
            pl.BlockSpec((tok, LANES), lambda step: (0, wide // LANES - 1)),
            pl.BlockSpec((tok, tile), lambda step: (0, jnp.minimum(step, tiles - 1))),
        ]
        + [anywhere()] * len(after),
        [columns(rows, tile), whole_block((2 * tok, rows))],
        [jax.ShapeDtypeStruct((rows, wide), BF16), jax.ShapeDtypeStruct((2 * tok, rows), BF16)],
        [pltpu.VMEM((rows, tok), BF16), pltpu.VMEM((rows, LANES), F32), pltpu.VMEM((rows, LANES), BF16)],
        payload,
        payload,
        *after,
        cost=cost,
    )


def stack_hidden(hidden_ref, spare_ref, out_ref, order):
    main = hidden_ref.shape[0] - spare_ref.shape[0]
    half = hidden_ref.shape[1] // 2
    core = lax.axis_index("dp")
    for at, flip in enumerate(order):
        start = pl.multiple_of((1 - core if flip else core) * half, LANES)
        out_ref[:main, at * half : (at + 1) * half] = hidden_ref[:main, pl.ds(start, half)]
        out_ref[main:, at * half : (at + 1) * half] = spare_ref[:, pl.ds(start, half)]


def out_kernel(hidden_ref, spare_ref, near_ref, far_ref, *rest):
    main_out, spare_out, stack_ref = rest[-3:]

    @pl.when(pl.program_id(0) == 0)
    def _():
        stack_hidden(hidden_ref, spare_ref, stack_ref, (False, True))

    main, half = main_out.shape[0], near_ref.shape[0]
    total = dot(stack_ref[:, :half], near_ref[...]) + dot(stack_ref[:, half:], far_ref[...])
    total = total.astype(BF16)
    main_out[...] = total[:main]
    spare_out[...] = total[main:]


def project(hidden, spare_hidden, near, far, tile, *after):
    half, width = near.shape
    slots, hid = hidden.shape
    spare = spare_hidden.shape[0]
    return call(
        out_kernel,
        width // tile,
        [whole_block(hidden.shape), whole_block(spare_hidden.shape), columns(half, tile), columns(half, tile)]
        + [anywhere()] * len(after),
        [columns(slots - spare, tile), columns(spare, tile)],
        [jax.ShapeDtypeStruct((slots - spare, width), BF16), jax.ShapeDtypeStruct((spare, width), BF16)],
        [pltpu.VMEM((slots, hid), BF16)],
        hidden,
        spare_hidden,
        near,
        far,
        *after,
    )


def slots_of(kind_ref, other_ref, second, main, spare):
    rows = kind_ref.shape[0]
    kind = kind_ref[...]
    lower = (iota((rows, rows), 1) < iota((rows, rows), 0)).astype(BF16)
    ahead = jnp.sum(other_ref[...].astype(F32), axis=0, keepdims=True)
    rank = dot(lower, kind) + jnp.where(second, ahead, 0.0)
    kind = kind.astype(F32)
    fits = lambda lane, limit: (kind[:, lane : lane + 1] > 0.5) & (rank[:, lane : lane + 1] < limit)
    slot = jnp.where(fits(1, spare), rank[:, 1:2] + (main + 1.0), 0.0)
    return jnp.where(fits(0, main), rank[:, 0:1] + 1.0, slot)


def upper_half(half):
    return lax.axis_index("expert") >= half


def give_kernel(half, mirrored, kind_ref, other_ref, main_ref, spare_ref, *rest):
    packed_ref, slot_ref = rest[-2:]
    rows, slots = slot_ref.shape
    main, spare = main_ref.shape[0], spare_ref.shape[0]

    @pl.when(pl.program_id(0) == 0)
    def _():
        second = upper_half(half) != mirrored
        slot = slots_of(kind_ref, other_ref, second, main, spare)
        slot_ref[...] = (iota((rows, slots), 1) + 1.0 == slot).astype(BF16)

    packed = dot(slot_ref[:, :main], main_ref[...]) + dot(slot_ref[:, main:], spare_ref[...])
    packed_ref[...] = packed.astype(BF16)


def kinds(arrived):
    rows, wide = arrived.shape
    return pl.BlockSpec((rows, LANES), lambda step: (0, wide // LANES - 1))


def give(arrived, other, out_main, out_spare, half, mirrored, tile, *after):
    main, width = out_main.shape
    spare = out_spare.shape[0]
    rows = arrived.shape[0]
    return call(
        functools.partial(give_kernel, half, mirrored),
        width // tile,
        [kinds(arrived), kinds(other), columns(main, tile), columns(spare, tile)]
        + [anywhere()] * len(after),
        columns(rows, tile),
        jax.ShapeDtypeStruct((rows, width), BF16),
        [pltpu.VMEM((rows, main + spare), BF16)],
        arrived,
        other,
        out_main,
        out_spare,
        *after,
    )


def mixed(mix_ref, rows_ref):
    both = dot(mix_ref[...], rows_ref[...])
    tok = both.shape[0] // 2
    return both[:tok] + both[tok:]


def part_kernel(mix_ref, rows_ref, part_ref):
    part_ref[...] = mixed(mix_ref, rows_ref).astype(BF16)


def total_kernel(mix_ref, rows_ref, other_ref, *rest):
    rest[-1][...] = (mixed(mix_ref, rows_ref) + other_ref[...].astype(F32)).astype(BF16)


def combine(mix, rows, other, tile, *after):
    count, width = rows.shape
    tok = mix.shape[0] // 2
    more = [] if other is None else [other]
    return call(
        part_kernel if other is None else total_kernel,
        width // tile,
        [whole_block(mix.shape), columns(count, tile)]
        + [columns(tok, tile)] * len(more)
        + [anywhere()] * len(after),
        columns(tok, tile),
        jax.ShapeDtypeStruct((tok, width), BF16),
        [],
        mix,
        rows,
        *more,
        *after,
    )


def slot_kernel(half, own_kind, mirror_kind, own_ref, mirror_ref, *rest):
    main_ref, spare_ref, own_slot, mirror_slot = rest[-4:]
    main, spare = main_ref.shape[0], spare_ref.shape[0]
    slots, rows = own_slot.shape

    @pl.when(pl.program_id(0) == 0)
    def _():
        upper = upper_half(half)
        pairs = (
            (own_kind, mirror_kind, upper, own_slot),
            (mirror_kind, own_kind, jnp.logical_not(upper), mirror_slot),
        )
        for kind, other, second, out_ref in pairs:
            slot = slots_of(kind, other, second, main, spare)
            slot = jnp.broadcast_to(slot, (rows, LANES)).T[0:1]
            out_ref[...] = (iota((slots, rows), 0) + 1.0 == slot).astype(BF16)

    total = dot(own_slot[...], own_ref[...]) + dot(mirror_slot[...], mirror_ref[...])
    total = total.astype(BF16)
    main_ref[...] = total[:main]
    spare_ref[...] = total[main:]


def to_slots(own, mirror, main, spare, half, tile, *after):
    rows, wide = own.shape
    width = wide - LANES
    return call(
        functools.partial(slot_kernel, half),
        width // tile,
        [kinds(own), kinds(mirror), columns(rows, tile), columns(rows, tile)] + [anywhere()] * len(after),
        [columns(main, tile), columns(spare, tile)],
        [jax.ShapeDtypeStruct((main, width), BF16), jax.ShapeDtypeStruct((spare, width), BF16)],
        [pltpu.VMEM((main + spare, rows), BF16), pltpu.VMEM((main + spare, rows), BF16)],
        own,
        mirror,
        own,
        mirror,
        *after,
    )


def weight_kernel(flip, with_other, hidden_ref, spare_ref, main_ref, grad_ref, *rest):
    out_ref, turned_ref, grads_ref = rest[-3:]
    main, half = main_ref.shape[0], turned_ref.shape[0]

    @pl.when(pl.program_id(0) == 0)
    def _():
        core = lax.axis_index("dp")
        start = pl.multiple_of((1 - core if flip else core) * half, LANES)
        turned_ref[:, :main] = hidden_ref[:main, pl.ds(start, half)].T
        turned_ref[:, main:] = spare_ref[:, pl.ds(start, half)].T

    grads_ref[:main] = main_ref[...]
    grads_ref[main:] = grad_ref[...]
    total = dot(turned_ref[...], grads_ref[...])
    if with_other:
        total = total + rest[0][...].astype(F32)
    out_ref[...] = total.astype(BF16)


def weight_part(hidden, spare_hidden, grads_main, grads_spare, other, flip, tile, *after):
    slots, hid = hidden.shape
    main, width = grads_main.shape
    spare = slots - main
    more = [] if other is None else [other]
    return call(
        functools.partial(weight_kernel, flip, bool(more)),
        width // tile,
        [whole_block(hidden.shape), whole_block(spare_hidden.shape), columns(main, tile), columns(spare, tile)]
        + [columns(hid // 2, tile)] * len(more)
        + [anywhere()] * len(after),
        columns(hid // 2, tile),
        jax.ShapeDtypeStruct((hid // 2, width), BF16),
        [pltpu.VMEM((hid // 2, slots), BF16), pltpu.VMEM((slots, tile), BF16)],
        hidden,
        spare_hidden,
        grads_main,
        grads_spare,
        *more,
        *after,
    )


def back_kernel(main_ref, spare_ref, near_ref, far_ref, main_out, spare_out, sum_ref):
    step = pl.program_id(0)
    core = lax.axis_index("dp")
    half = near_ref.shape[0]

    @pl.when(step == 0)
    def _():
        sum_ref[...] = jnp.zeros_like(sum_ref)

    main = main_ref.shape[0]
    for at, weight in ((0, near_ref), (half, far_ref)):
        sum_ref[:main, at : at + half] += dot(main_ref[...], weight[...], 1, 1)
        sum_ref[main:, at : at + half] += dot(spare_ref[...], weight[...], 1, 1)

    @pl.when(step == pl.num_programs(0) - 1)
    def _():
        near = pl.multiple_of(core * half, LANES)
        far = pl.multiple_of((1 - core) * half, LANES)
        for start, at in ((near, 0), (far, half)):
            total = sum_ref[:, at : at + half].astype(BF16)
            main_out[:, pl.ds(start, half)] = total[:main]
            spare_out[:, pl.ds(start, half)] = total[main:]


def project_back(grads_main, grads_spare, near, far, tile):
    main, width = grads_main.shape
    spare = grads_spare.shape[0]
    half = near.shape[0]
    return call(
        back_kernel,
        width // tile,
        [columns(main, tile), columns(spare, tile), columns(half, tile), columns(half, tile)],
        [whole_block((main, 2 * half)), whole_block((spare, 2 * half))],
        [jax.ShapeDtypeStruct((main, 2 * half), BF16), jax.ShapeDtypeStruct((spare, 2 * half), BF16)],
        [pltpu.VMEM((main + spare, 2 * half), F32)],
        grads_main,
        grads_spare,
        near,
        far,
    )


def local(hidden_saved, down_weight, route_device, replica_flag, gate_values, grad_out):
    count = lax.axis_size("expert")
    half = count // 2
    tok, top = route_device.shape
    width = grad_out.shape[1]
    cap = 5 * tok * top // (4 * count)
    main = 3 * tok * top // 4
    hidden = hidden_saved[0, 0]
    near = down_weight[0]
    tile = width // 4
    groups = [list(range(half)), list(range(half, count))]

    def to_half(rows):
        return lax.all_to_all(
            rows.reshape(half, cap, -1), "expert", 0, 0, axis_index_groups=groups, tiled=True
        ).reshape(half * cap, -1)

    payload, spare_hidden = head(
        route_device.T, replica_flag.T, gate_values.T, grad_out, hidden, hidden.shape[0] - main
    )
    mirror = swapped(payload, "expert", half)
    far = swapped(near, "dp", 1)
    spare_hidden = swapped(spare_hidden, "expert", half)
    packed_own, mix_own = pack(payload, cap, top, half, tile, 0)
    arrived_own = to_half(packed_own)
    out_main, out_spare = project(hidden, spare_hidden, near, far, tile, mix_own)
    packed_mirror, mix_mirror = pack(mirror, cap, top, half, tile, LONG, out_spare)
    out_spare = swapped(out_spare, "expert", half)
    arrived_mirror = to_half(packed_mirror)
    given_mirror = give(arrived_mirror, arrived_own, out_main, out_spare, half, True, tile)
    returned_mirror = to_half(given_mirror)
    grads_main, grads_spare = to_slots(
        arrived_own, arrived_mirror, main, hidden.shape[0] - main, half, tile, given_mirror
    )
    given_own = give(arrived_own, arrived_mirror, out_main, out_spare, half, False, tile, grads_spare)
    returned_own = to_half(given_own)
    grads_spare = swapped(grads_spare, "expert", half)
    part = combine(mix_mirror, returned_mirror, None, tile)
    far_part = weight_part(hidden, spare_hidden, grads_main, grads_spare, None, True, tile, part)
    part = swapped(part, "expert", half)
    far_part = swapped(far_part, "dp", 1)
    back_main, back_spare = project_back(grads_main, grads_spare, near, far, tile)
    back_spare = swapped(back_spare, "expert", half)
    grad_weight = weight_part(hidden, spare_hidden, grads_main, grads_spare, far_part, False, tile)
    layer_out = combine(mix_own, returned_own, part, tile, grad_weight)
    grad_hidden = jnp.concatenate([back_main, back_spare], axis=0)
    return (layer_out, grad_hidden[None, None], grad_weight[None])


def solution(mesh):
    in_specs = (
        P("dp", "expert", None, None),
        P("expert", "dp", None),
        P(("dp", "expert"), None),
        P(("dp", "expert"), None),
        P(("dp", "expert"), None),
        P(("dp", "expert"), None),
    )
    out_specs = (P(("dp", "expert"), None), P("dp", "expert", None, None), P("expert", "dp", None))
    return jax.shard_map(local, mesh=mesh, in_specs=in_specs, out_specs=out_specs, check_vma=False)
```

time: 259 us -> 256 us (0.988)
  Pallas kernels: 48.9 us -> 71 us
  local copies, waits for them, and re-layouts: 15.6 us -> 6.87 us
  waiting for transfers between devices: 150 us -> 142 us
  starting transfers between devices: 39.7 us -> 32.7 us
    pallas_call x11 -> x12, Pallas kernels: 48.9 us -> 71 us  [call(): pl.pallas_call(body, grid=(grid,), in_specs=in_specs, out_specs=out_specs...]
    unnamed x37 -> x16, local copies, waits for them, and re-layouts: 14.1 us -> 6.87 us
    all_to_all x5 -> x4, starting transfers between devices: 31.7 us -> 24.7 us  [to_half(): lax.all_to_all(rows.reshape(half, cap, -1), 'expert', 0, 0, axis_index_gr...]
    ppermute x8, waiting for transfers between devices: 123 us -> 118 us  [swapped(): return lax.ppermute(value, axis, pairs)]
    all_to_all x5 -> x4, waiting for transfers between devices: 27.8 us -> 24 us  [to_half(): lax.all_to_all(rows.reshape(half, cap, -1), 'expert', 0, 0, axis_index_gr...]
  transfers between devices with their start and end apart: 13 -> 12, of which waited for: 6 -> 5; matrix products, arithmetic and copies ran while one was open for 1% -> 1% of each run, Pallas kernels for 17% -> 21%
where the time goes in v1:
time: 256 us; the launch traced here: 255 us
  waiting for transfers between devices  142 us (55%)
  Pallas kernels  71 us (28%)
  starting transfers between devices  32.7 us (13%)
  local copies, waits for them, and re-layouts  6.87 us (3%)
    ppermute x8, waiting for transfers between devices, swapped(): return lax.ppermute(value, axis, pairs)  118 us
    pallas_call x12, Pallas kernels, call(): pl.pallas_call(body, grid=(grid,), in_specs=in_specs, out_specs=out_specs...  71 us
    all_to_all x4, starting transfers between devices, to_half(): lax.all_to_all(rows.reshape(half, cap, -1), 'expert', 0, 0, axis_index_gr...  24.7 us
    all_to_all x4, waiting for transfers between devices, to_half(): lax.all_to_all(rows.reshape(half, cap, -1), 'expert', 0, 0, axis_index_gr...  24 us
    ppermute x8, starting transfers between devices, swapped(): return lax.ppermute(value, axis, pairs)  8.04 us
    unnamed x16, local copies, waits for them, and re-layouts  6.87 us
  transfers between devices with their start and end apart: 12, of which 5 were waited for; matrix products, arithmetic and copies ran while one was open for 1% of the time, Pallas kernels for 21%

profile of v1, /device:TPU:0, one launch (start us, length us, event | category | flops | bytes accessed | tf_op | source)
XLA Modules:
  0.0 255.0 jit_solution(13322445809862516889)
XLA Ops:
  0.6 2.3 shard_map.85
  2.9 5.0 %shard_map.86 = (bf16[320,3712]{1,0:T(8,128)(2,1)}, bf16[256,320]{1,0:T(8,128)(2,1)}) custom-call(bf16[128,3712]{1,0:T(8,128)(2,1)} %get-tuple-element.15.meta_ref.tokens_ref, bf16[128,3712]{1,0:T(8,128)(2,1)} %get-tuple-element.15.meta_ref.tokens_ref), custom_call_target="tpu_custom_call" | custom-call | tf_op jit(solution)/shard_map/pallas_call | solution.py:41
  7.9 6.2 %all-to-all-start = ((bf16[8,40,3712]{2,1,0:T(8,128)(2,1)}), bf16[8,40,3712]{2,1,0:T(8,128)(2,1)S(1)}, u32[]{:S(2)}, u32[]{:S(2)}) async-start(bf16[8,40,3712]{2,1,0:T(8,128)(2,1)} %bitcast.32), calls=%async_computation | async-start | bytes 4751360 | tf_op jit(solution)/shard_map/all_to_all | solution.py:450
  14.1 0.0 collective-permute-start.2
  14.1 2.7 %collective-permute-start = (bf16[128,3712]{1,0:T(8,128)(2,1)}, bf16[128,3712]{1,0:T(8,128)(2,1)S(1)}, u32[]{:S(2)}, u32[]{:S(2)}) collective-permute-start(bf16[128,3712]{1,0:T(8,128)(2,1)} %get-tuple-element.15.meta_ref.tokens_ref), channel_id=1, source_target_pairs={{0,8},{1,9},{2,10},{3,11},{4,12},{5,13},{6,14},{7,15},{8,0},{9,1},... | collective-permute-start | bytes 2850824 | tf_op jit(solution)/shard_map/ppermute | solution.py:18
  16.8 0.3 collective-permute-start.1
  17.1 46.1 %collective-permute-done.1.spare_ref = bf16[64,1024]{1,0:T(8,128)(2,1)S(1)} collective-permute-done((bf16[64,1024]{1,0:T(8,128)(2,1)}, bf16[64,1024]{1,0:T(8,128)(2,1)S(1)}, u32[]{:S(2)}, u32[]{:S(2)}) %collective-permute-start.1) | collective-permute-done | bytes 131104 | tf_op jit(solution)/shard_map/ppermute | solution.py:18
  63.2 0.0 copy-start.6
  63.2 0.0 collective-permute-done.2.far_ref
  63.2 0.6 copy-done.6
  63.8 8.0 %shard_map.87 = (bf16[384,3584]{1,0:T(8,128)(2,1)}, bf16[64,3584]{1,0:T(8,128)(2,1)}) custom-call(bf16[448,1024]{1,0:T(8,128)(2,1)} %bitcast.22, bf16[64,1024]{1,0:T(8,128)(2,1)} %copy-done.6, bf16[512,3584]{1,0:T(8,128)(2,1)} %bitcast.26, bf16[512,3584]{1,0:T(8,128)(2,1)} %collective-permute-done.2.far_ref, bf16[256,320]{1,0:T(8,128)(2,1)} %get-tuple-element.16.rest_0_.mix_ref), custom_call_target="tpu_custom_call" | custom-call | tf_op jit(solution)/shard_map/pallas_call | solution.py:41
  71.8 0.0 collective-permute-done.meta_ref.tokens_ref
  71.8 0.0 copy-start.4
  71.8 0.9 copy-done.4
  72.7 5.0 %shard_map.88 = (bf16[320,3712]{1,0:T(8,128)(2,1)}, bf16[256,320]{1,0:T(8,128)(2,1)}) custom-call(bf16[128,3712]{1,0:T(8,128)(2,1)} %copy-done.4, bf16[128,3712]{1,0:T(8,128)(2,1)} %copy-done.4, bf16[64,3584]{1,0:T(8,128)(2,1)} %get-tuple-element.19.rest_0_), custom_call_target="tpu_custom_call" | custom-call | bytes 400000000 | tf_op jit(solution)/shard_map/pallas_call | solution.py:41
  77.8 0.0 all-to-all-done
  77.8 0.0 copy-start
  77.8 1.5 copy-done
  79.3 10.9 %all-to-all-start.1 = ((bf16[8,40,3712]{2,1,0:T(8,128)(2,1)}), bf16[8,40,3712]{2,1,0:T(8,128)(2,1)}, u32[]{:S(2)}, u32[]{:S(2)}) async-start(bf16[8,40,3712]{2,1,0:T(8,128)(2,1)} %bitcast.33), calls=%async_computation.1 | async-start | bytes 4751360 | tf_op jit(solution)/shard_map/all_to_all | solution.py:450
  90.2 0.0 collective-permute-start.3
  90.2 34.5 %collective-permute-done.3.spare_ref = bf16[64,3584]{1,0:T(8,128)(2,1)S(1)} collective-permute-done((bf16[64,3584]{1,0:T(8,128)(2,1)}, bf16[64,3584]{1,0:T(8,128)(2,1)S(1)}, u32[]{:S(2)}, u32[]{:S(2)}) %collective-permute-start.3) | collective-permute-done | bytes 458784 | tf_op jit(solution)/shard_map/ppermute | solution.py:18
  124.7 0.0 copy-start.5
  124.7 3.2 %all-to-all-done.1 = bf16[8,40,3712]{2,1,0:T(8,128)(2,1)} async-done(((bf16[8,40,3712]{2,1,0:T(8,128)(2,1)}), bf16[8,40,3712]{2,1,0:T(8,128)(2,1)}, u32[]{:S(2)}, u32[]{:S(2)}) %all-to-all-start.1) | async-done | bytes 2375712 | tf_op jit(solution)/shard_map/all_to_all | solution.py:450
  127.9 0.0 copy-done.5
  127.9 5.6 %shard_map.89.rest_0_ = bf16[320,3584]{1,0:T(8,128)(2,1)} custom-call(bf16[320,3712]{1,0:T(8,128)(2,1)} %bitcast.8.kind_ref.mirror_kind.mirror_ref.other_ref, bf16[320,3712]{1,0:T(8,128)(2,1)} %bitcast.16, bf16[384,3584]{1,0:T(8,128)(2,1)} %get-tuple-element.21.main_ref, bf16[64,3584]{1,0:T(8,128)(2,1)} %copy-done.5), custom_call_target="tpu_custom_call" | custom-call | tf_op jit(solution)/shard_map/pallas_call | solution.py:41
  133.6 3.6 %all-to-all-start.3 = ((bf16[8,40,3584]{2,1,0:T(8,128)(2,1)}), bf16[8,40,3584]{2,1,0:T(8,128)(2,1)S(1)}, u32[]{:S(2)}, u32[]{:S(2)}) async-start(bf16[8,40,3584]{2,1,0:T(8,128)(2,1)} %bitcast.20), calls=%async_computation.3 | async-start | bytes 4587520 | tf_op jit(solution)/shard_map/all_to_all | solution.py:450
  137.2 7.8 %shard_map.90 = (bf16[384,3584]{1,0:T(8,128)(2,1)}, bf16[64,3584]{1,0:T(8,128)(2,1)}) custom-call(bf16[320,3712]{1,0:T(8,128)(2,1)} %bitcast.17, bf16[320,3712]{1,0:T(8,128)(2,1)} %bitcast.8.kind_ref.mirror_kind.mirror_ref.other_ref, bf16[320,3712]{1,0:T(8,128)(2,1)} %bitcast.18, bf16[320,3712]{1,0:T(8,128)(2,1)} %bitcast.8.kind_ref.mirror_kind.mirror_ref.other_ref, ...), custom_call_target="tpu_custom_call" | custom-call | tf_op jit(solution)/shard_map/pallas_call | solution.py:41
  145.0 2.1 collective-permute-start.5
  147.1 5.6 %shard_map.91 = bf16[320,3584]{1,0:T(8,128)(2,1)} custom-call(bf16[320,3712]{1,0:T(8,128)(2,1)} %bitcast.19, bf16[320,3712]{1,0:T(8,128)(2,1)} %bitcast.8.kind_ref.mirror_kind.mirror_ref.other_ref, bf16[384,3584]{1,0:T(8,128)(2,1)} %get-tuple-element.21.main_ref, bf16[64,3584]{1,0:T(8,128)(2,1)} %copy-done.5, bf16[64,3584]{1,0:T(8,128)(2,1)} %get-tuple-element.22.rest_0_), custom_call_target="tpu_custom_call" | custom-call | tf_op jit(solution)/shard_map/pallas_call | solution.py:41
  152.7 20.7 %all-to-all-done.3 = bf16[8,40,3584]{2,1,0:T(8,128)(2,1)S(1)} async-done(((bf16[8,40,3584]{2,1,0:T(8,128)(2,1)}), bf16[8,40,3584]{2,1,0:T(8,128)(2,1)S(1)}, u32[]{:S(2)}, u32[]{:S(2)}) %all-to-all-start.3) | async-done | bytes 2293792 | tf_op jit(solution)/shard_map/all_to_all | solution.py:450
  173.4 0.0 copy-start.2
  173.4 1.4 copy-done.2
  174.8 4.0 %all-to-all-start.2 = ((bf16[8,40,3584]{2,1,0:T(8,128)(2,1)}), bf16[8,40,3584]{2,1,0:T(8,128)(2,1)S(1)}, u32[]{:S(2)}, u32[]{:S(2)}) async-start(bf16[8,40,3584]{2,1,0:T(8,128)(2,1)} %bitcast.31), calls=%async_computation.2 | async-start | bytes 4587520 | tf_op jit(solution)/shard_map/all_to_all | solution.py:450
  178.8 4.4 %shard_map.92.rest_0_ = bf16[128,3584]{1,0:T(8,128)(2,1)} custom-call(bf16[256,320]{1,0:T(8,128)(2,1)} %get-tuple-element.23.mix_ref, bf16[320,3584]{1,0:T(8,128)(2,1)} %bitcast.30), custom_call_target="tpu_custom_call" | custom-call | tf_op jit(solution)/shard_map/pallas_call | solution.py:41
  183.2 0.0 collective-permute-done.5.grad_ref.spare_ref
  183.2 0.0 copy-start.3
  183.2 0.8 copy-done.3
  184.0 6.3 %shard_map.93 = bf16[512,3584]{1,0:T(8,128)(2,1)} custom-call(bf16[448,1024]{1,0:T(8,128)(2,1)} %bitcast.23, bf16[64,1024]{1,0:T(8,128)(2,1)} %copy-done.6, bf16[384,3584]{1,0:T(8,128)(2,1)} %get-tuple-element.24.main_ref, bf16[64,3584]{1,0:T(8,128)(2,1)} %copy-done.3, bf16[128,3584]{1,0:T(8,128)(2,1)} %shard_map.92.rest_0_), custom_call_target="tpu_custom_call" | custom-call | tf_op jit(solution)/shard_map/pallas_call | solution.py:41
  190.3 0.0 collective-permute-start.6
  190.3 0.1 collective-permute-start.4
  190.4 9.2 %shard_map.96 = (bf16[384,1024]{1,0:T(8,128)(2,1)}, bf16[64,1024]{1,0:T(8,128)(2,1)}) custom-call(bf16[384,3584]{1,0:T(8,128)(2,1)} %get-tuple-element.24.main_ref, bf16[64,3584]{1,0:T(8,128)(2,1)} %copy-done.3, bf16[512,3584]{1,0:T(8,128)(2,1)} %bitcast.27, bf16[512,3584]{1,0:T(8,128)(2,1)} %collective-permute-done.2.far_ref), custom_call_target="tpu_custom_call" | custom-call | tf_op jit(solution)/shard_map/pallas_call | solution.py:41
  199.6 2.8 %collective-permute-start.7 = (bf16[64,1024]{1,0:T(8,128)(2,1)}, bf16[64,1024]{1,0:T(8,128)(2,1)S(1)}, u32[]{:S(2)}, u32[]{:S(2)}) collective-permute-start(bf16[64,1024]{1,0:T(8,128)(2,1)} %get-tuple-element.26), channel_id=1, source_target_pairs={{0,8},{1,9},{2,10},{3,11},{4,12},{5,13},{6,14},{7,15},{8,0},{9,1},... | collective-permute-start | bytes 393224 | tf_op jit(solution)/shard_map/ppermute | solution.py:18
  202.4 37.1 %collective-permute-done.7 = bf16[64,1024]{1,0:T(8,128)(2,1)S(1)} collective-permute-done((bf16[64,1024]{1,0:T(8,128)(2,1)}, bf16[64,1024]{1,0:T(8,128)(2,1)S(1)}, u32[]{:S(2)}, u32[]{:S(2)}) %collective-permute-start.7) | collective-permute-done | bytes 131104 | tf_op jit(solution)/shard_map/ppermute | solution.py:18
  239.5 2.1 maximum_bitcast_fusion
  241.6 0.0 collective-permute-done.6.rest_0_
  241.6 7.2 %shard_map.94.rest_0_ = bf16[512,3584]{1,0:T(8,128)(2,1)} custom-call(bf16[448,1024]{1,0:T(8,128)(2,1)} %bitcast.24, bf16[64,1024]{1,0:T(8,128)(2,1)} %copy-done.6, bf16[384,3584]{1,0:T(8,128)(2,1)} %get-tuple-element.24.main_ref, bf16[64,3584]{1,0:T(8,128)(2,1)} %copy-done.3, bf16[512,3584]{1,0:T(8,128)(2,1)} %collective-permute-done.6.rest_0_), custom_call_target="tpu_custom_call" | custom-call | tf_op jit(solution)/shard_map/pallas_call | solution.py:41
  248.8 0.0 all-to-all-done.2
  248.8 0.0 copy-start.1
  248.8 0.0 collective-permute-done.4.other_ref
  248.8 0.0 copy-start.7
  248.8 1.4 copy-done.1
  250.2 0.3 copy-done.7
  250.5 4.5 %shard_map.95 = bf16[128,3584]{1,0:T(8,128)(2,1)} custom-call(bf16[256,320]{1,0:T(8,128)(2,1)} %get-tuple-element.16.rest_0_.mix_ref, bf16[320,3584]{1,0:T(8,128)(2,1)} %bitcast.29, bf16[128,3584]{1,0:T(8,128)(2,1)} %copy-done.7, bf16[512,3584]{1,0:T(8,128)(2,1)} %shard_map.94.rest_0_), custom_call_target="tpu_custom_call" | custom-call | tf_op jit(solution)/shard_map/pallas_call | solution.py:41
Async XLA Ops:
  7.9 69.8 %all-to-all-start = ((bf16[8,40,3712]{2,1,0:T(8,128)(2,1)}), bf16[8,40,3712]{2,1,0:T(8,128)(2,1)S(1)}, u32[]{:S(2)}, u32[]{:S(2)}) async-start(bf16[8,40,3712]{2,1,0:T(8,128)(2,1)} %bitcast.32), calls=%async_computation | async-start | bytes 4751360 | tf_op jit(solution)/shard_map/all_to_all | solution.py:450
  14.1 49.1 %collective-permute-start.2 = (bf16[512,3584]{1,0:T(8,128)(2,1)}, bf16[512,3584]{1,0:T(8,128)(2,1)}, u32[]{:S(2)}, u32[]{:S(2)}) collective-permute-start(bf16[512,3584]{1,0:T(8,128)(2,1)} %bitcast.25), channel_id=1, source_target_pairs={{0,16},{16,0},{1,17},{17,1},{2,18},{18,2},{3,19},{19,3},{4,20},{20... | collective-permute-start | bytes 11010056 | tf_op jit(solution)/shard_map/ppermute | solution.py:18
  14.1 57.7 %collective-permute-start = (bf16[128,3712]{1,0:T(8,128)(2,1)}, bf16[128,3712]{1,0:T(8,128)(2,1)S(1)}, u32[]{:S(2)}, u32[]{:S(2)}) collective-permute-start(bf16[128,3712]{1,0:T(8,128)(2,1)} %get-tuple-element.15.meta_ref.tokens_ref), channel_id=1, source_target_pairs={{0,8},{1,9},{2,10},{3,11},{4,12},{5,13},{6,14},{7,15},{8,0},{9,1},... | collective-permute-start | bytes 2850824 | tf_op jit(solution)/shard_map/ppermute | solution.py:18
  16.8 46.4 %collective-permute-start.1 = (bf16[64,1024]{1,0:T(8,128)(2,1)}, bf16[64,1024]{1,0:T(8,128)(2,1)S(1)}, u32[]{:S(2)}, u32[]{:S(2)}) collective-permute-start(bf16[64,1024]{1,0:T(8,128)(2,1)} %get-tuple-element.18), channel_id=1, source_target_pairs={{0,8},{1,9},{2,10},{3,11},{4,12},{5,13},{6,14},{7,15},{8,0},{9,1},... | collective-permute-start | bytes 393224 | tf_op jit(solution)/shard_map/ppermute | solution.py:18
  63.2 0.6 copy-start.6
  71.8 0.9 copy-start.4
  77.8 1.5 copy-start
  79.3 48.7 %all-to-all-start.1 = ((bf16[8,40,3712]{2,1,0:T(8,128)(2,1)}), bf16[8,40,3712]{2,1,0:T(8,128)(2,1)}, u32[]{:S(2)}, u32[]{:S(2)}) async-start(bf16[8,40,3712]{2,1,0:T(8,128)(2,1)} %bitcast.33), calls=%async_computation.1 | async-start | bytes 4751360 | tf_op jit(solution)/shard_map/all_to_all | solution.py:450
  90.2 34.5 %collective-permute-start.3 = (bf16[64,3584]{1,0:T(8,128)(2,1)}, bf16[64,3584]{1,0:T(8,128)(2,1)S(1)}, u32[]{:S(2)}, u32[]{:S(2)}) collective-permute-start(bf16[64,3584]{1,0:T(8,128)(2,1)} %get-tuple-element.19.rest_0_), channel_id=1, source_target_pairs={{0,8},{1,9},{2,10},{3,11},{4,12},{5,13},{6,14},{7,15},{8,0},{9,1},... | collective-permute-start | bytes 1376264 | tf_op jit(solution)/shard_map/ppermute | solution.py:18
  124.7 3.2 %copy-start.5 = (bf16[64,3584]{1,0:T(8,128)(2,1)}, bf16[64,3584]{1,0:T(8,128)(2,1)S(1)}, u32[]{:S(2)}) copy-start(bf16[64,3584]{1,0:T(8,128)(2,1)S(1)} %collective-permute-done.3.spare_ref) | copy-start | bytes 1376260
  133.6 39.9 %all-to-all-start.3 = ((bf16[8,40,3584]{2,1,0:T(8,128)(2,1)}), bf16[8,40,3584]{2,1,0:T(8,128)(2,1)S(1)}, u32[]{:S(2)}, u32[]{:S(2)}) async-start(bf16[8,40,3584]{2,1,0:T(8,128)(2,1)} %bitcast.20), calls=%async_computation.3 | async-start | bytes 4587520 | tf_op jit(solution)/shard_map/all_to_all | solution.py:450
  145.0 38.2 %collective-permute-start.5 = (bf16[64,3584]{1,0:T(8,128)(2,1)}, bf16[64,3584]{1,0:T(8,128)(2,1)S(1)}, u32[]{:S(2)}, u32[]{:S(2)}) collective-permute-start(bf16[64,3584]{1,0:T(8,128)(2,1)} %get-tuple-element.22.rest_0_), channel_id=1, source_target_pairs={{0,8},{1,9},{2,10},{3,11},{4,12},{5,13},{6,14},{7,15},{8,0},{9,1},... | collective-permute-start | bytes 1376264 | tf_op jit(solution)/shard_map/ppermute | solution.py:18
  173.4 1.4 copy-start.2
  174.8 74.0 %all-to-all-start.2 = ((bf16[8,40,3584]{2,1,0:T(8,128)(2,1)}), bf16[8,40,3584]{2,1,0:T(8,128)(2,1)S(1)}, u32[]{:S(2)}, u32[]{:S(2)}) async-start(bf16[8,40,3584]{2,1,0:T(8,128)(2,1)} %bitcast.31), calls=%async_computation.2 | async-start | bytes 4587520 | tf_op jit(solution)/shard_map/all_to_all | solution.py:450
  183.2 0.8 copy-start.3
  190.3 51.3 %collective-permute-start.6 = (bf16[512,3584]{1,0:T(8,128)(2,1)}, bf16[512,3584]{1,0:T(8,128)(2,1)}, u32[]{:S(2)}, u32[]{:S(2)}) collective-permute-start(bf16[512,3584]{1,0:T(8,128)(2,1)} %shard_map.93), channel_id=1, source_target_pairs={{0,16},{16,0},{1,17},{17,1},{2,18},{18,2},{3,19},{19,3},{4,20},{20... | collective-permute-start | bytes 11010056 | tf_op jit(solution)/shard_map/ppermute | solution.py:18
  190.3 58.5 %collective-permute-start.4 = (bf16[128,3584]{1,0:T(8,128)(2,1)}, bf16[128,3584]{1,0:T(8,128)(2,1)S(1)}, u32[]{:S(2)}, u32[]{:S(2)}) collective-permute-start(bf16[128,3584]{1,0:T(8,128)(2,1)} %shard_map.92.rest_0_), channel_id=1, source_target_pairs={{0,8},{1,9},{2,10},{3,11},{4,12},{5,13},{6,14},{7,15},{8,0},{9,1},... | collective-permute-start | bytes 2752520 | tf_op jit(solution)/shard_map/ppermute | solution.py:18
  199.6 39.9 %collective-permute-start.7 = (bf16[64,1024]{1,0:T(8,128)(2,1)}, bf16[64,1024]{1,0:T(8,128)(2,1)S(1)}, u32[]{:S(2)}, u32[]{:S(2)}) collective-permute-start(bf16[64,1024]{1,0:T(8,128)(2,1)} %get-tuple-element.26), channel_id=1, source_target_pairs={{0,8},{1,9},{2,10},{3,11},{4,12},{5,13},{6,14},{7,15},{8,0},{9,1},... | collective-permute-start | bytes 393224 | tf_op jit(solution)/shard_map/ppermute | solution.py:18
  248.8 1.4 copy-start.1
  248.8 1.7 copy-start.7
